TPU v7x, 256 devices: a whole 4x4x8 slice. The times are simulated.
256 devices in a mesh: row: 64 (over x, z, core), col: 4 (over y).
Axes of the slice: x: 4, y: 4, z: 8, core: 2. Of those that a mesh axis runs over, the one named last changes fastest.
Arguments:
- matrix: float32 [65536, 4096], P('row', 'col'), may hold values from -80 to 80, as said below
Outputs:
- q_panels: float32 [65536, 512], P('row')
- coeff_rows: float32 [512, 4096], P(None, 'col')
- remainder: float32 [65536, 4096], P('row', 'col')
Inputs may be any that keep to these rules, and one draw needn't show every extreme that they name: `matrix`: the first 512 columns have full column rank; the other columns are well conditioned against them.
All inputs are finite; a program needn't handle non-finite values.
Results may differ from a plain program's by a relative error of at most 0.0003.
Values sent between devices are 32-bit elements; how exact they have to be, the bound alone decides.
A program may use at most 64 MiB of HBM per device.

v0:
```python
import jax
import jax.numpy as jnp
from jax import lax
from jax.sharding import PartitionSpec as P

PW = 256


def rows_for(lines, count):
    spare = -len(lines) % count
    return jnp.pad(lines, [(0, spare)] + [(0, 0)] * (lines.ndim - 1))


def broadcast_by_parts(array, axis, root):
    lines = jnp.where(lax.axis_index(axis) == root, array, jnp.zeros_like(array)).reshape(
        -1, *array.shape[1:][-1:]
    )
    padded = rows_for(lines, lax.axis_size(axis))
    own = lax.psum_scatter(padded, axis, scatter_dimension=0, tiled=True)
    return lax.all_gather(own, axis, axis=0, tiled=True)[: len(lines)].reshape(array.shape)


def inverse_factor(gram_matrix):
    factor_low = jnp.linalg.cholesky(gram_matrix)
    identity = jnp.eye(gram_matrix.shape[0], dtype=jnp.float32)
    return jax.scipy.linalg.solve_triangular(factor_low, identity, lower=True)


def inner_products(factor_left, factor_right):
    return lax.dot_general(
        factor_left,
        factor_right,
        (((0,), (0,)), ((), ())),
        precision=lax.Precision.HIGHEST,
        preferred_element_type=jnp.float32,
    )


def apply_inverse(panel_cols, inverse):
    return lax.dot_general(
        panel_cols,
        inverse,
        (((1,), (1,)), ((), ())),
        precision=lax.Precision.HIGHEST,
        preferred_element_type=jnp.float32,
    )


def combine(basis, coeff_part):
    return jnp.dot(
        basis, coeff_part, precision=lax.Precision.HIGHEST, preferred_element_type=jnp.float32
    )


def on_device(matrix):
    row_count = matrix.shape[0] * lax.axis_size("row")
    width = PW
    local_block = matrix
    panels = broadcast_by_parts(local_block[:, : 2 * width], "col", 0)
    gram_sum, cross_sum = lax.psum(
        (inner_products(panels, panels), inner_products(panels, local_block)), "row"
    )
    inverse = inverse_factor(gram_sum / row_count)
    q_panels = apply_inverse(panels, inverse)
    coeff_rows = jnp.dot(
        inverse,
        cross_sum / row_count,
        precision=lax.Precision.HIGHEST,
        preferred_element_type=jnp.float32,
    )
    local_block = local_block - combine(q_panels, coeff_rows)
    return (q_panels, coeff_rows, local_block)


def solution(mesh):
    return jax.shard_map(
        on_device,
        mesh=mesh,
        in_specs=(P("row", "col"),),
        out_specs=(P("row", None), P(None, "col"), P("row", "col")),
        check_vma=False,
    )
```

profile of v0, /device:TPU:9, one launch (start us, length us, event | category | flops | bytes accessed | tf_op | source)
XLA Modules:
  0.0 466.7 jit_solution(14064841441922526498)
XLA Ops:
  7.2 3.1 slice_select_fusion
  10.4 34.7 %reduce-scatter.2.cloned.1.call-done = f32[256,512]{1,0:T(8,128)} async-done(((f32[1024,512]{1,0:T(8,128)}), f32[256,512]{1,0:T(8,128)}) %reduce-scatter.2.cloned.1.call-update) | async-done | bytes 524304 | tf_op jit(solution)/shard_map/reduce_scatter | solution.py:19
  45.2 35.3 %all-gather.2.cloned.1.call-done = f32[1024,512]{1,0:T(8,128)} async-done(((f32[256,512]{1,0:T(8,128)}), f32[1024,512]{1,0:T(8,128)}) %all-gather.2.cloned.1.call-update) | async-done | bytes 2097168 | tf_op jit(solution)/shard_map/all_gather | solution.py:20
  80.4 11.1 %fusion.40 = f32[512,1024]{1,0:T(8,128)} fusion(f32[1024,512]{1,0:T(8,128)} %all-gather.2.cloned.1.call-done, f32[1024,1024]{1,0:T(8,128)} %param.1), kind=kOutput, calls=%fused_computation.80 | convolution fusion | flops 6442450944 | bytes 8388608 | tf_op jit(solution)/shard_map/dot_general | solution.py:30
  91.5 4.5 fusion.39
  98.0 190.2 %all-reduce.4.cloned.1.call-done = (f32[512,512]{0,1:T(8,128)}, f32[512,1024]{1,0:T(8,128)}) async-done(((f32[512,512]{0,1:T(8,128)}, f32[512,1024]{1,0:T(8,128)}), (f32[512,512]{0,1:T(8,128)}, f32[512,1024]{1,0:T(8,128)})) %all-reduce.4.cloned.1.call-update) | async-done | bytes 3145744 | tf_op jit(solution)/shard_map/psum | solution.py:60
  288.2 2.4 broadcast_multiply_fusion
  290.6 2.5 copy.5
  293.1 1.5 fusion.2
  295.5 11.7 %cholesky.104 = f32[128,128]{1,0:T(8,128)S(1)} custom-call(f32[128,128]{1,0:T(8,128)S(1)} %cholesky.266), custom_call_target="Cholesky" | custom-call | tf_op jit(solution)/shard_map/jit(cholesky)/cholesky | solution.py:24
  307.3 9.8 %custom-call.31 = f32[1,128,128]{1,2,0:T(8,128)S(1)} custom-call(f32[1,128,128]{2,1,0:T(8,128)S(1)} %get-tuple-element.32), custom_call_target="InvertDiagBlocksLowerTriangular" | custom-call | tf_op jit(solution)/shard_map/jit(cholesky)/cholesky | solution.py:24
  317.2 1.2 constant_dynamic-update-slice_fusion.3
  318.5 1.3 convolution_subtract_fusion.4
  319.8 11.9 %cholesky.217 = f32[128,128]{1,0:T(8,128)S(1)} custom-call(f32[128,128]{1,0:T(8,128)S(1)} %cholesky.270), custom_call_target="Cholesky" | custom-call | tf_op jit(solution)/shard_map/jit(cholesky)/cholesky | solution.py:24
  331.7 9.8 %custom-call.32 = f32[1,128,128]{1,2,0:T(8,128)S(1)} custom-call(f32[1,128,128]{2,1,0:T(8,128)S(1)} %get-tuple-element.29), custom_call_target="InvertDiagBlocksLowerTriangular" | custom-call | tf_op jit(solution)/shard_map/jit(cholesky)/cholesky | solution.py:24
  341.8 1.3 convolution_subtract_fusion.5
  343.1 11.7 %cholesky.238 = f32[128,128]{1,0:T(8,128)S(1)} custom-call(f32[128,128]{1,0:T(8,128)S(1)} %cholesky.275), custom_call_target="Cholesky" | custom-call | tf_op jit(solution)/shard_map/jit(cholesky)/cholesky | solution.py:24
  355.5 9.8 %custom-call.33 = f32[1,128,128]{1,2,0:T(8,128)S(1)} custom-call(f32[1,128,128]{2,1,0:T(8,128)S(1)} %get-tuple-element.26), custom_call_target="InvertDiagBlocksLowerTriangular" | custom-call | tf_op jit(solution)/shard_map/jit(cholesky)/cholesky | solution.py:24
  365.5 1.2 convolution_subtract_fusion.6
  366.7 11.9 %cholesky.255 = f32[128,128]{1,0:T(8,128)S(1)} custom-call(f32[128,128]{1,0:T(8,128)S(1)} %convolution_subtract_fusion.6), custom_call_target="Cholesky" | custom-call | tf_op jit(solution)/shard_map/jit(cholesky)/cholesky | solution.py:24
  383.6 13.9 %while.1 = (s32[]{:T(128)}, f32[512,512]{1,0:T(8,128)}, s32[4,2]{0,1:T(2,128)S(1)}, f32[4,128,128]{2,1,0:T(8,128)}, s32[]{:T(128)}) while((s32[]{:T(128)}, f32[512,512]{1,0:T(8,128)}, s32[4,2]{0,1:T(2,128)S(1)}, f32[4,128,128]{2,1,0:T(8,128)}, s32[]{:T(128)}) %tuple.31), condition=%wide.while_cond, body=%wide.while_body.sunk | while | flops 2 | bytes 132705 | solution.py:26
  384.2 2.9 bitcast_dynamic-update-slice_fusion.2
  387.7 2.9 bitcast_dynamic-update-slice_fusion.2
  391.1 2.9 bitcast_dynamic-update-slice_fusion.2
  394.6 2.8 bitcast_dynamic-update-slice_fusion.2
  397.4 40.1 %custom-call.34 = f32[4,128,128]{1,2,0:T(8,128)S(1)} custom-call(f32[4,128,128]{2,1,0:T(8,128)} %get-tuple-element.10), custom_call_target="InvertDiagBlocksLowerTriangular" | custom-call | tf_op jit(solution)/shard_map/jit(_solve_triangular)/triangular_solve | solution.py:26
  438.7 1.4 convolution_subtract_fusion.2
  440.5 1.5 convolution_subtract_fusion.1
  442.4 1.6 convolution_subtract_fusion.3
  444.4 3.6 fusion
  448.0 3.5 fusion.9
  451.5 8.4 %convolution_subtract_fusion = f32[1024,1024]{1,0:T(8,128)} fusion(f32[1024,1024]{1,0:T(8,128)S(1)} %copy-done.1, f32[1024,512]{1,0:T(8,128)S(1)} %fusion.9, f32[512,1024]{1,0:T(8,128)S(1)} %fusion), kind=kOutput, calls=%fused_computation.2 | convolution fusion | flops 6443499520 | bytes 12582912 | tf_op jit(solution)/shard_map/dot_general | solution.py:50
  (53 shorter events, 11.6 us)
Async XLA Ops:
  7.2 37.9 %reduce-scatter.2.cloned.1.call-start = ((), (), s32[]{:S(2)}) async-start(), calls=%async_computation.1 | async-start | bytes 2621440 | tf_op jit(solution)/shard_map/reduce_scatter | solution.py:19
  10.4 70.1 %all-gather.2.cloned.1.call-start = ((), (), s32[]{:S(2)}) async-start(), calls=%async_computation.2 | async-start | bytes 2621440 | tf_op jit(solution)/shard_map/all_gather | solution.py:20
  45.1 243.1 %all-reduce.4.cloned.1.call-start = ((), (), s32[]{:S(2)}) async-start(), calls=%async_computation.3 | async-start | bytes 6291456 | tf_op jit(solution)/shard_map/psum | solution.py:60
  80.4 11.1 %copy-start = (f32[1024,512]{1,0:T(8,128)S(1)}, f32[1024,512]{1,0:T(8,128)}, u32[]{:S(2)}) copy-start(f32[1024,512]{1,0:T(8,128)} %all-gather.2.cloned.1.call-done) | copy-start | bytes 6291460
  288.2 4.9 %copy-start.4 = (f32[512,512]{0,1:T(8,128)S(1)}, f32[512,512]{0,1:T(8,128)}, u32[]{:S(2)}) copy-start(f32[512,512]{0,1:T(8,128)} %get-tuple-element.19) | copy-start | bytes 3145732
  294.6 1.0 copy-start.6
  383.6 56.9 %copy-start.5 = (f32[512,512]{1,0:T(8,128)S(1)}, f32[512,512]{1,0:T(8,128)}, u32[]{:S(2)}) copy-start(f32[512,512]{1,0:T(8,128)} %fusion.13) | copy-start | bytes 3145732
  440.0 4.4 copy-start.7
  448.0 3.5 copy-start.2
  448.0 3.5 copy-start.1
  451.5 8.4 %copy-start.3 = (f32[1024,512]{1,0:T(8,128)}, f32[1024,512]{1,0:T(8,128)S(1)}, u32[]{:S(2)}) copy-start(f32[1024,512]{1,0:T(8,128)S(1)} %fusion.9) | copy-start | bytes 6291460
Sparse Core Ops, SparseCore 0:
  11.1 33.9 reduce-scatter.1
  47.0 33.3 all-gather.1
  96.2 191.9 all-reduce.3
where the time goes:
time: 472 us; the launch traced here: 467 us
  waiting for transfers between devices  260 us (55%)
  other arithmetic  129 us (27%)
  matrix products  43.2 us (9%)
  local copies, waits for them, and re-layouts  17.5 us (4%)
  between operations  16.8 us (4%)
    psum x1, waiting for transfers between devices, on_device(): lax.psum((inner_products(panels, panels), inner_products(panels, local_bl...  190 us
    another operation x14, other arithmetic, inverse_factor(): factor_low = jnp.linalg.cholesky(gram_matrix)  78.7 us
    another operation x3, other arithmetic, inverse_factor(): return jax.scipy.linalg.solve_triangular(factor_low, identity, lower=True)  41.2 us
    all_gather x1, waiting for transfers between devices, broadcast_by_parts(): lax.all_gather(own, axis, axis=0, tiled=True)[:len(lines)]  35.3 us
    reduce_scatter x1, waiting for transfers between devices, broadcast_by_parts(): own = lax.psum_scatter(padded, axis, scatter_dimension=0, tiled=True)  34.7 us
    dot_general x2, matrix products, inner_products(): lax.dot_general(factor_left, factor_right, (((0,), (0,)), ((), ())), prec...  15.6 us
    another operation x12, local copies, waits for them, and re-layouts  13.8 us
  transfers between devices with their start and end apart: 3, of which 3 were waited for; matrix products, arithmetic and copies ran while one was open for 0% of the time, Pallas kernels for 0%

commit v1 on v0

v1 whole, which is shorter than its diff:
```python
import functools

import jax
import jax.numpy as jnp
from jax import lax
from jax.experimental import pallas as pl
from jax.experimental.pallas import tpu as pltpu
from jax.sharding import PartitionSpec as P

MESH = pl.DeviceIdType.MESH
F32, BF16 = jnp.float32, jnp.bfloat16
X, Z, Y = 4, 8, 4
N, NB = 512, 128
CHUNKS = 4
SUBS = 8
PART = 256
BLOCKS = [(i, j) for j in range(4) for i in range(j, 4)]
GROUPS = 16 * len(BLOCKS)


def split(value):
    high = value.astype(BF16)
    return high, (value - high.astype(F32)).astype(BF16)


def dot3(left, right, dims):
    dot = functools.partial(
        lax.dot_general, dimension_numbers=(dims, ((), ())), preferred_element_type=F32
    )
    return dot(left[0], right[0]) + (dot(left[0], right[1]) + dot(left[1], right[0]))


def dot_full(left, right, dims):
    return lax.dot_general(
        left, right, (dims, ((), ())), precision=lax.Precision.HIGHEST, preferred_element_type=F32
    )


def leaf(tiles):
    lane = lax.broadcasted_iota(jnp.int32, (8, 128), 1)
    sub = lax.broadcasted_iota(jnp.int32, (8, 128), 0)
    tiles = list(tiles)
    for r in range(16):
        lo = 8 * r
        group = (lane >= lo) & (lane < lo + 8)
        cols = {
            i: [jnp.broadcast_to(tiles[i][:, lo + m : lo + m + 1], (8, 128)) for m in range(8)]
            for i in range(r, 16)
        }
        pivot = {
            (i, m): jnp.broadcast_to(cols[r][m][i : i + 1, :], (8, 128))
            for m in range(8)
            for i in range(m, 8)
        }
        base = jnp.where(group, (lane - lo == sub).astype(F32), tiles[r])
        rows = [jnp.broadcast_to(base[m : m + 1, :], (8, 128)) for m in range(8)]
        for i in range(r + 1, 16):
            tiles[i] = jnp.where(group, 0.0, tiles[i])
        out = jnp.zeros((8, 128), F32)
        for j in range(8):
            inv = lax.rsqrt(pivot[j, j])
            low = {m: pivot[m, j] * inv for m in range(j + 1, 8)}
            for m in range(j + 1, 8):
                for i in range(m, 8):
                    pivot[i, m] = pivot[i, m] - low[i] * low[m]
            row = rows[j] * inv
            for m in range(j + 1, 8):
                rows[m] = rows[m] - low[m] * row
            out = jnp.where(sub == j, row, out)
            for i in range(r + 1, 16):
                col = cols[i][j] * inv
                for m in range(j + 1, 8):
                    cols[i][m] = cols[i][m] - col * low[m]
                tiles[i] = tiles[i] - col * row
        tiles[r] = jnp.where(lane <= sub + lo, out, 0.0)
    return tiles


def factor(gram, inv):
    inv[...] = jnp.zeros_like(inv)
    for k in range(4):
        a, b = k * NB, (k + 1) * NB
        own = jnp.concatenate(leaf([gram[a + 8 * i : a + 8 * i + 8, a:b] for i in range(16)]), axis=0)
        inv[a:b, a:b] = own
        if k:
            inv[a:b, :a] = dot_full(own, inv[a:b, :a], ((1,), (0,)))
        if k < 3:
            low = dot_full(gram[b:, a:b], own, ((1,), (1,)))
            gram[b:, b:] = gram[b:, b:] - dot_full(low, low, ((1,), (1,)))
            inv[b:, :b] = inv[b:, :b] - dot_full(low, inv[a:b, :b], ((1,), (0,)))


def gather_kernel(
    rows_total, a_hbm, p_out, c_out, g_out,
    a, a_hi, a_lo, p, c_own, c_sib, c_x, c_s, c_z, c_all,
    g_own, g_sib, g_x, g_s, g_z, g_all,
    load_sem, store_sem, p_send, p_recv, cs_send, cs_recv, cx_send, cx_recv, cz_send, cz_recv,
    caz_send, caz_recv, cax_send, cax_recv, ce_send, ce_recv, gs_send, gs_recv, gx_send, gx_recv,
    gz_send, gz_recv, gy_send, gy_recv, gaz_send, gaz_recv, gax_send, gax_recv, ge_send, ge_recv,
):
    row, y = lax.axis_index("row"), lax.axis_index("col")
    core, z, x = row % 2, (row // 2) % Z, row // (2 * Z)
    piece = x * Z + z

    def at(px, py, pz, pc):
        return ((px * Z + pz) * 2 + pc, py)

    def x_peer(i):
        return (x + i) % X

    def z_peer(i):
        return (z + i) % Z

    def remote(src, dst, send, recv, device):
        return pltpu.make_async_remote_copy(
            src_ref=src, dst_ref=dst, send_sem=send, recv_sem=recv, device_id=device, device_id_type=MESH
        )

    sibling = at(x, y, z, 1 - core)
    barrier = pltpu.get_barrier_semaphore()
    friends = [sibling]
    friends += [at(x_peer(i), y, z, core) for i in range(1, X)]
    friends += [at(x, y, z_peer(i), core) for i in range(1, Z)]
    friends += [at(x, (y + i) % Y, z, core) for i in range(1, Y)]
    for friend in friends:
        pl.semaphore_signal(barrier, inc=1, device_id=friend, device_id_type=MESH)

    def p_copy(way, s, step):
        rows = pl.ds(512 * way + PART * (s % 2), PART)
        part = p.at[s // 2, rows, :]
        return remote(part, part, p_send.at[way, s], p_recv.at[way, s], at(x, (y + step) % Y, z, core))

    def up(s):
        return p_copy(0, s, 1)

    def down(s):
        return p_copy(1, s, Y - 1)

    def cs(k):
        return [remote(c_own.at[k], c_sib.at[k], cs_send.at[k], cs_recv.at[k], sibling)]

    def cx(k):
        return [
            remote(
                c_own.at[k, pl.ds(x_peer(i) * Z, Z)], c_x.at[k, i - 1],
                cx_send.at[k, i - 1], cx_recv.at[k, i - 1], at(x_peer(i), y, z, core),
            )
            for i in range(1, X)
        ]

    def cz(k):
        return [
            remote(
                c_s.at[k, z_peer(i)], c_z.at[k, i - 1],
                cz_send.at[k, i - 1], cz_recv.at[k, i - 1], at(x, y, z_peer(i), core),
            )
            for i in range(1, Z)
        ]

    def caz(k):
        return [
            remote(
                c_all.at[k, piece], c_all.at[k, piece],
                caz_send.at[k, i - 1], caz_recv.at[k, i - 1], at(x, y, z_peer(i), core),
            )
            for i in range(1, Z)
        ]

    def cax(k):
        own = c_all.at[k, pl.ds(x * Z, Z)]
        return [
            remote(own, own, cax_send.at[k, i - 1], cax_recv.at[k, i - 1], at(x_peer(i), y, z, core))
            for i in range(1, X)
        ]

    def ce(k):
        return [remote(c_all.at[k], c_all.at[k], ce_send.at[k], ce_recv.at[k], sibling)]

    five, forty = GROUPS // (X * Z), GROUPS // X

    def gs():
        return [remote(g_own, g_sib, gs_send, gs_recv, sibling)]

    def gx():
        return [
            remote(
                g_own.at[pl.ds(x_peer(i) * forty, forty)], g_x.at[i - 1],
                gx_send.at[i - 1], gx_recv.at[i - 1], at(x_peer(i), y, z, core),
            )
            for i in range(1, X)
        ]

    def gz():
        return [
            remote(
                g_s.at[pl.ds(z_peer(i) * five, five)], g_z.at[i - 1],
                gz_send.at[i - 1], gz_recv.at[i - 1], at(x, y, z_peer(i), core),
            )
            for i in range(1, Z)
        ]

    g_piece = g_all.at[pl.ds(piece * five, five)]

    def gy():
        return [
            remote(g_piece, g_piece, gy_send.at[i - 1], gy_recv, at(x, (y + i) % Y, z, core))
            for i in range(1, Y)
        ]

    def gaz():
        return [
            remote(g_piece, g_piece, gaz_send.at[i - 1], gaz_recv.at[i - 1], at(x, y, z_peer(i), core))
            for i in range(1, Z)
        ]

    def gax():
        own = g_all.at[pl.ds(x * forty, forty)]
        return [
            remote(own, own, gax_send.at[i - 1], gax_recv.at[i - 1], at(x_peer(i), y, z, core))
            for i in range(1, X)
        ]

    def ge():
        return [remote(g_all, g_all, ge_send, ge_recv, sibling)]

    def start(copies):
        for copy in copies:
            copy.start()

    def arrive(copies):
        for copy in copies:
            copy.wait_recv()

    def sent(copies):
        for copy in copies:
            copy.wait_send()

    def p_load(k):
        return pltpu.make_async_copy(a_hbm.at[:, pl.ds(NB * k, NB)], p.at[k], load_sem.at[1 + k])

    a_load = pltpu.make_async_copy(a_hbm, a, load_sem.at[0])

    @pl.when(y == 0)
    def _():
        for k in range(CHUNKS):
            p_load(k).start()

    a_load.start()

    @pl.when(y == 0)
    def _():
        for k in range(CHUNKS):
            p_load(k).wait()

    pl.semaphore_wait(barrier, len(friends))

    @pl.when(y == 0)
    def _():
        for s in range(SUBS):
            up(s).start()
            down(s).start()
        flipped = [split(p[k].T) for k in range(CHUNKS)]
        for b, (i, j) in enumerate(BLOCKS):
            block = dot3(flipped[i], flipped[j], ((1,), (1,)))
            for r in range(16):
                g_own[16 * b + r] = block[8 * r : 8 * r + 8, :]

        @pl.when(core == 0)
        def _():
            start(gs())

        @pl.when(core == 1)
        def _():
            arrive(gs())
            g_own[...] = g_own[...] + g_sib[...]
            start(gx())

    a_load.wait()
    for r in range(0, 1024, 256):
        high, low = split(a[r : r + 256, :])
        a_hi[r : r + 256, :] = high
        a_lo[r : r + 256, :] = low

    def p_step(t):
        @pl.when(y == 1)
        def _():
            if t < SUBS:
                up(t).wait_recv()
                up(t).start()
            if 0 <= t - 2 < SUBS:
                down(t - 2).wait_recv()

        @pl.when(y == 2)
        def _():
            if 0 <= t - 1 < SUBS:
                up(t - 1).wait_recv()
                up(t - 1).start()
                down(t - 1).wait_recv()
                down(t - 1).start()

        @pl.when(y == 3)
        def _():
            if t < SUBS:
                down(t).wait_recv()
                down(t).start()
            if 0 <= t - 2 < SUBS:
                up(t - 2).wait_recv()

    def p_store(k):
        return pltpu.make_async_copy(p.at[k], p_out.at[k], store_sem.at[k])

    def compute(k):
        left = split(p[k].T)
        for tile in range(4):
            lanes = slice(256 * tile, 256 * tile + 256)
            part = dot3(left, (a_hi[:, lanes], a_lo[:, lanes]), ((1,), (0,)))
            half, inner = tile // 2, slice(256 * (tile % 2), 256 * (tile % 2) + 256)
            for r in range(16):
                c_own[k, 2 * r + half, :, inner] = part[8 * r : 8 * r + 8, :]
        p_store(k).start()

    def c_stage(k, stage):
        if not 0 <= k < CHUNKS:
            return
        if stage == 1:
            arrive(cs(k))
            c_own[k] = c_own[k] + c_sib[k]
            start(cx(k))
        elif stage == 2:
            arrive(cx(k))
            c_s[k] = c_own[k, pl.ds(x * Z, Z)] + c_x[k, 0] + (c_x[k, 1] + c_x[k, 2])
            start(cz(k))
        elif stage == 3:
            arrive(cz(k))
            total = c_s[k, z]
            for i in range(Z - 1):
                total = total + c_z[k, i]
            c_all[k, piece] = total * (1.0 / rows_total)
            start(caz(k))
        elif stage == 4:
            arrive(caz(k))
            start(cax(k))
        elif stage == 5:
            arrive(cax(k))
            start(ce(k))

    def g_stage(t):
        if t == 4:

            @pl.when(y == 0)
            def _():
                arrive(gx())
                g_s[...] = g_own[pl.ds(x * forty, forty)] + g_x[0] + (g_x[1] + g_x[2])
                start(gz())

        if t == 6:

            @pl.when(y == 0)
            def _():
                arrive(gz())
                total = g_s[pl.ds(z * five, five)]
                for i in range(Z - 1):
                    total = total + g_z[i]
                g_all[pl.ds(piece * five, five)] = total * (1.0 / rows_total)
                start(gy())

        if t == 8:

            @pl.when(y != 0)
            def _():
                gy()[0].wait_recv()

            start(gaz())
        if t == 10:
            arrive(gaz())
            start(gax())
        if t == 12:
            arrive(gax())
            start(ge())

    for t in range(14):
        p_step(t)
        ready = (t - 3) // 2
        fresh = t >= 3 and t % 2 == 1 and ready < CHUNKS
        if fresh:
            compute(ready)

        @pl.when(core == 1)
        def _():
            if fresh:
                start(cs(ready))
            g_stage(t)

        @pl.when(core == 0)
        def _():
            if fresh:
                c_stage(ready, 1)
            for stage in range(5, 1, -1):
                if (t - stage - 2) % 2 == 0:
                    c_stage((t - stage - 2) // 2, stage)

    g_store = pltpu.make_async_copy(g_all, g_out, store_sem.at[4])

    def c_store(k):
        return pltpu.make_async_copy(c_all.at[k], c_out.at[k], store_sem.at[5 + k])

    @pl.when(core == 0)
    def _():
        for k in range(CHUNKS):
            c_store(k).start()
        arrive(ge())
        g_store.start()

    @pl.when(core == 1)
    def _():
        g_store.start()
        for k in range(CHUNKS):
            arrive(ce(k))
            c_store(k).start()

    @pl.when((y == 0) | (y == 1) | (y == 2))
    def _():
        for s in range(SUBS):
            up(s).wait_send()

    @pl.when((y == 0) | (y == 2) | (y == 3))
    def _():
        for s in range(SUBS):
            down(s).wait_send()

    @pl.when(core == 0)
    def _():
        @pl.when(y == 0)
        def _():
            sent(gs())

        for k in range(CHUNKS):
            sent(cx(k) + cz(k) + caz(k) + cax(k) + ce(k))

    @pl.when(core == 1)
    def _():
        @pl.when(y == 0)
        def _():
            sent(gx() + gz() + gy())

        for k in range(CHUNKS):
            sent(cs(k))
        sent(gaz() + gax() + ge())

    for k in range(CHUNKS):
        p_store(k).wait()
        c_store(k).wait()
    g_store.wait()


def factor_kernel(groups, inv, gram):
    for b, (i, j) in enumerate(BLOCKS):
        for r in range(16):
            gram[NB * i + 8 * r : NB * i + 8 * r + 8, NB * j : NB * j + NB] = groups[16 * b + r]
    factor(gram, inv)


def finish_kernel(a, p, inv, c, q, coeff, rest, inv_hi, inv_lo, coeff_hi, coeff_lo):
    half = N // 2

    @pl.when(pl.program_id(0) == 0)
    def _():
        high, low = split(inv[...])
        inv_hi[...] = high
        inv_lo[...] = low
        for tile in range(2):
            lanes = slice(512 * tile, 512 * tile + 512)
            sums = [
                jnp.concatenate([c[k, 2 * r + tile] for k in ks for r in range(16)], axis=0)
                for ks in ((0, 1), (2, 3))
            ]
            right = split(jnp.concatenate(sums, axis=0))
            upper = dot3(
                (high[:half, :half], low[:half, :half]), (right[0][:half], right[1][:half]), ((1,), (0,))
            )
            lower = dot3((high[half:], low[half:]), right, ((1,), (0,)))
            for start, part in ((0, upper), (half, lower)):
                coeff[start : start + half, lanes] = part
                part_hi, part_lo = split(part)
                coeff_hi[start : start + half, lanes] = part_hi
                coeff_lo[start : start + half, lanes] = part_lo

    panels = split(jnp.concatenate([p[k] for k in range(CHUNKS)], axis=1))
    upper = dot3(
        (panels[0][:, :half], panels[1][:, :half]),
        (inv_hi[:half, :half], inv_lo[:half, :half]),
        ((1,), (1,)),
    )
    lower = dot3(panels, (inv_hi[half:, :], inv_lo[half:, :]), ((1,), (1,)))
    basis = jnp.concatenate([upper, lower], axis=1)
    q[...] = basis
    left = split(basis)
    for tile in range(2):
        lanes = slice(512 * tile, 512 * tile + 512)
        rest[:, lanes] = a[:, lanes] - dot3(left, (coeff_hi[:, lanes], coeff_lo[:, lanes]), ((1,), (0,)))


def vmem(*shape, dtype=F32):
    return pltpu.VMEM(shape, dtype)


def dma(*shape):
    return pltpu.SemaphoreType.DMA(shape) if shape else pltpu.SemaphoreType.DMA


def on_device(matrix):
    rows_total = matrix.shape[0] * lax.axis_size("row")
    any_space = pl.BlockSpec(memory_space=pl.ANY)
    five, forty = GROUPS // (X * Z), GROUPS // X
    pairs = [
        (2, SUBS), (4,), (4, 3), (4, 7), (4, 7), (4, 3), (4,), (), (3,), (7,),
    ]
    sems = [dma(*shape) for shape in pairs for _ in range(2)]
    panels, sums, groups = pl.pallas_call(
        functools.partial(gather_kernel, rows_total),
        out_shape=(
            jax.ShapeDtypeStruct((4, 1024, NB), F32),
            jax.ShapeDtypeStruct((4, 32, 8, 512), F32),
            jax.ShapeDtypeStruct((GROUPS, 8, 128), F32),
        ),
        in_specs=[any_space],
        out_specs=[any_space] * 3,
        scratch_shapes=[
            vmem(1024, 1024), vmem(1024, 1024, dtype=BF16), vmem(1024, 1024, dtype=BF16),
            vmem(4, 1024, NB), vmem(4, 32, 8, 512), vmem(4, 32, 8, 512), vmem(4, 3, 8, 8, 512),
            vmem(4, 8, 8, 512), vmem(4, 7, 8, 512), vmem(4, 32, 8, 512),
            vmem(GROUPS, 8, 128), vmem(GROUPS, 8, 128), vmem(3, forty, 8, 128), vmem(forty, 8, 128),
            vmem(7, five, 8, 128), vmem(GROUPS, 8, 128),
            dma(5), dma(9), *sems,
            dma(3), dma(), dma(7), dma(7), dma(3), dma(3), dma(), dma(),
        ],
        compiler_params=pltpu.CompilerParams(
            collective_id=0, has_side_effects=True, vmem_limit_bytes=56 * 1024 * 1024
        ),
        name="gather",
    )(matrix)
    inverse = pl.pallas_call(
        factor_kernel,
        out_shape=jax.ShapeDtypeStruct((N, N), F32),
        in_specs=[pl.BlockSpec(memory_space=pltpu.VMEM)],
        out_specs=pl.BlockSpec(memory_space=pltpu.VMEM),
        scratch_shapes=[vmem(N, N)],
        compiler_params=pltpu.CompilerParams(vmem_limit_bytes=32 * 1024 * 1024),
        name="factor",
    )(groups)
    tile = 256
    return pl.pallas_call(
        finish_kernel,
        grid=(1024 // tile,),
        out_shape=(
            jax.ShapeDtypeStruct((1024, N), F32),
            jax.ShapeDtypeStruct((N, 1024), F32),
            jax.ShapeDtypeStruct((1024, 1024), F32),
        ),
        in_specs=[
            pl.BlockSpec((tile, 1024), lambda i: (i, 0)),
            pl.BlockSpec((4, tile, NB), lambda i: (0, i, 0)),
            pl.BlockSpec((N, N), lambda i: (0, 0)),
            pl.BlockSpec((4, 32, 8, 512), lambda i: (0, 0, 0, 0)),
        ],
        out_specs=[
            pl.BlockSpec((tile, N), lambda i: (i, 0)),
            pl.BlockSpec((N, 1024), lambda i: (0, 0)),
            pl.BlockSpec((tile, 1024), lambda i: (i, 0)),
        ],
        scratch_shapes=[
            vmem(N, N, dtype=BF16), vmem(N, N, dtype=BF16),
            vmem(N, 1024, dtype=BF16), vmem(N, 1024, dtype=BF16),
        ],
        compiler_params=pltpu.CompilerParams(vmem_limit_bytes=48 * 1024 * 1024),
        name="finish",
    )(matrix, panels, inverse, sums)


def solution(mesh):
    return jax.shard_map(
        on_device,
        mesh=mesh,
        in_specs=(P("row", "col"),),
        out_specs=(P("row", None), P(None, "col"), P("row", "col")),
        check_vma=False,
    )
```

time: 472 us -> 129 us (0.27); the launches traced: 467 us -> 129 us
  waiting for transfers between devices: 260 us -> 0 us
  other arithmetic: 129 us -> 0 us
  Pallas kernels: 0 us -> 124 us
  matrix products: 43.2 us -> 0 us
  between operations: 16.8 us -> 0.66 us
  local copies, waits for them, and re-layouts: 17.5 us -> 4.26 us
    psum x1 -> x0, waiting for transfers between devices: 190 us -> none  [on_device(): lax.psum((inner_products(panels, panels), inner_products(panels, local_bl...]
    pallas_call x0 -> x3, Pallas kernels: none -> 124 us  [the longest x1 93.2 us: on_device(): pl.pallas_call(functools.partial(gather_kernel, rows_total), out_shape=(j...]
    another operation x17 -> x0, other arithmetic: 120 us -> none  [the longest x14 78.7 us: inverse_factor(): factor_low = jnp.linalg.cholesky(gram_matrix)]
    all_gather x1 -> x0, waiting for transfers between devices: 35.3 us -> none  [broadcast_by_parts(): lax.all_gather(own, axis, axis=0, tiled=True)[:len(lines)]]
    reduce_scatter x1 -> x0, waiting for transfers between devices: 34.7 us -> none  [broadcast_by_parts(): own = lax.psum_scatter(padded, axis, scatter_dimension=0, tiled=True)]
    dot_general x5 -> x0, matrix products: 31 us -> none  [the longest x2 15.6 us: inner_products(): lax.dot_general(factor_left, factor_right, (((0,), (0,)), ((), ())), prec...]
    another operation x17 -> x0, local copies, waits for them, and re-layouts: 14 us -> none
    another operation x13 -> x0, matrix products: 12.2 us -> none  [the longest x7 6.78 us: inverse_factor(): return jax.scipy.linalg.solve_triangular(factor_low, identity, lower=True)]
  transfers between devices with their start and end apart: 3 -> 0, of which waited for: 3 -> 0; matrix products, arithmetic and copies ran while one was open for 0% -> 0% of each run, Pallas kernels for 0% -> 0%
where the time goes in v1:
time: 129 us
  Pallas kernels  124 us (96%)
  local copies, waits for them, and re-layouts  4.26 us (3%)
    pallas_call x1, Pallas kernels, on_device(): pl.pallas_call(functools.partial(gather_kernel, rows_total), out_shape=(j...  93.2 us
    pallas_call x1, Pallas kernels, on_device(): pl.pallas_call(factor_kernel, out_shape=jax.ShapeDtypeStruct((N, N), F32)...  21 us
    pallas_call x1, Pallas kernels, on_device(): pl.pallas_call(finish_kernel, grid=(1024 // tile,), out_shape=(jax.ShapeD...  9.6 us
    unnamed x6, local copies, waits for them, and re-layouts  4.26 us

profile of v1, /device:TPU:9, one launch (start us, length us, event | category | flops | bytes accessed | tf_op | source)
XLA Modules:
  0.0 128.8 jit_solution(7631769929409063392)
XLA Ops:
  0.6 93.2 %gather.1 = (f32[4,1024,128]{2,1,0:T(8,128)}, f32[4,32,8,512]{3,2,1,0:T(8,128)}, f32[160,8,128]{2,1,0:T(8,128)}) custom-call(f32[1024,1024]{1,0:T(8,128)} %a.1), custom_call_target="tpu_custom_call" | custom-call | tf_op jit(solution)/shard_map/gather/pallas_call | solution.py:519
  93.9 0.0 copy-start.2
  93.9 1.1 copy-done.2
  94.9 21.0 %factor.1.inv = f32[512,512]{1,0:T(8,128)S(1)} custom-call(f32[160,8,128]{2,1,0:T(8,128)S(1)} %copy-done.2), custom_call_target="tpu_custom_call" | custom-call | tf_op jit(solution)/shard_map/factor/pallas_call | solution.py:542
  116.0 0.0 copy-start
  116.0 1.6 %copy-done = f32[4,1024,128]{2,1,0:T(8,128)S(1)} copy-done((f32[4,1024,128]{2,1,0:T(8,128)S(1)}, f32[4,1024,128]{2,1,0:T(8,128)}, u32[]{:S(2)}) %copy-start) | copy-done | bytes 2097176
  117.6 0.0 copy-start.1
  117.6 1.6 %copy-done.1 = f32[4,32,8,512]{3,2,1,0:T(8,128)S(1)} copy-done((f32[4,32,8,512]{3,2,1,0:T(8,128)S(1)}, f32[4,32,8,512]{3,2,1,0:T(8,128)}, u32[]{:S(2)}) %copy-start.1) | copy-done | bytes 2097176
  119.2 9.6 %finish.1 = (f32[1024,512]{1,0:T(8,128)}, f32[512,1024]{1,0:T(8,128)}, f32[1024,1024]{1,0:T(8,128)}) custom-call(f32[1024,1024]{1,0:T(8,128)} %a.1, f32[4,1024,128]{2,1,0:T(8,128)S(1)} %copy-done, f32[512,512]{1,0:T(8,128)S(1)} %factor.1.inv, f32[4,32,8,512]{3,2,1,0:T(8,128)S(1)} %copy-done.1), custom_call_target="tpu_custom_call" | custom-call | tf_op jit(solution)/shard_map/finish/pallas_call | solution.py:552
Async XLA Ops:
  93.9 1.1 copy-start.2
  116.0 1.6 %copy-start = (f32[4,1024,128]{2,1,0:T(8,128)S(1)}, f32[4,1024,128]{2,1,0:T(8,128)}, u32[]{:S(2)}) copy-start(f32[4,1024,128]{2,1,0:T(8,128)} %get-tuple-element.6.p) | copy-start | bytes 6291460
  117.6 1.6 %copy-start.1 = (f32[4,32,8,512]{3,2,1,0:T(8,128)S(1)}, f32[4,32,8,512]{3,2,1,0:T(8,128)}, u32[]{:S(2)}) copy-start(f32[4,32,8,512]{3,2,1,0:T(8,128)} %get-tuple-element.8.c) | copy-start | bytes 6291460

commit v2 on v1

--- a/solution.py
+++ b/solution.py
@@ -76,7 +76,7 @@
     return tiles
 
 
-def factor(gram, inv):
+def factor(gram, inv, done):
     inv[...] = jnp.zeros_like(inv)
     for k in range(4):
         a, b = k * NB, (k + 1) * NB
@@ -84,6 +84,7 @@
         inv[a:b, a:b] = own
         if k:
             inv[a:b, :a] = dot_full(own, inv[a:b, :a], ((1,), (0,)))
+        done(k)
         if k < 3:
             low = dot_full(gram[b:, a:b], own, ((1,), (1,)))
             gram[b:, b:] = gram[b:, b:] - dot_full(low, low, ((1,), (1,)))
@@ -91,9 +92,9 @@
 
 
 def gather_kernel(
-    rows_total, a_hbm, p_out, c_out, g_out,
+    rows_total, a_hbm, p_out, c_out, inv_out,
     a, a_hi, a_lo, p, c_own, c_sib, c_x, c_s, c_z, c_all,
-    g_own, g_sib, g_x, g_s, g_z, g_all,
+    g_own, g_sib, g_x, g_s, g_z, g_all, gram, inv,
     load_sem, store_sem, p_send, p_recv, cs_send, cs_recv, cx_send, cx_recv, cz_send, cz_recv,
     caz_send, caz_recv, cax_send, cax_recv, ce_send, ce_recv, gs_send, gs_recv, gx_send, gx_recv,
     gz_send, gz_recv, gy_send, gy_recv, gaz_send, gaz_recv, gax_send, gax_recv, ge_send, ge_recv,
@@ -220,8 +221,9 @@
             for i in range(1, X)
         ]
 
-    def ge():
-        return [remote(g_all, g_all, ge_send, ge_recv, sibling)]
+    def ge(k):
+        rows = inv.at[pl.ds(NB * k, NB)]
+        return [remote(rows, rows, ge_send.at[k], ge_recv.at[k], sibling)]
 
     def start(copies):
         for copy in copies:
@@ -376,7 +378,10 @@
             start(gax())
         if t == 12:
             arrive(gax())
-            start(ge())
+            for b, (i, j) in enumerate(BLOCKS):
+                for r in range(16):
+                    gram[NB * i + 8 * r : NB * i + 8 * r + 8, NB * j : NB * j + NB] = g_all[16 * b + r]
+            factor(gram, inv, lambda k: start(ge(k)))
 
     for t in range(14):
         p_step(t)
@@ -399,7 +404,7 @@
                 if (t - stage - 2) % 2 == 0:
                     c_stage((t - stage - 2) // 2, stage)
 
-    g_store = pltpu.make_async_copy(g_all, g_out, store_sem.at[4])
+    inv_store = pltpu.make_async_copy(inv, inv_out, store_sem.at[4])
 
     def c_store(k):
         return pltpu.make_async_copy(c_all.at[k], c_out.at[k], store_sem.at[5 + k])
@@ -408,12 +413,13 @@
     def _():
         for k in range(CHUNKS):
             c_store(k).start()
-        arrive(ge())
-        g_store.start()
+        for k in range(4):
+            arrive(ge(k))
+        inv_store.start()
 
     @pl.when(core == 1)
     def _():
-        g_store.start()
+        inv_store.start()
         for k in range(CHUNKS):
             arrive(ce(k))
             c_store(k).start()
@@ -445,19 +451,13 @@
 
         for k in range(CHUNKS):
             sent(cs(k))
-        sent(gaz() + gax() + ge())
+            sent(ge(k))
+        sent(gaz() + gax())
 
     for k in range(CHUNKS):
         p_store(k).wait()
         c_store(k).wait()
-    g_store.wait()
-
-
-def factor_kernel(groups, inv, gram):
-    for b, (i, j) in enumerate(BLOCKS):
-        for r in range(16):
-            gram[NB * i + 8 * r : NB * i + 8 * r + 8, NB * j : NB * j + NB] = groups[16 * b + r]
-    factor(gram, inv)
+    inv_store.wait()
 
 
 def finish_kernel(a, p, inv, c, q, coeff, rest, inv_hi, inv_lo, coeff_hi, coeff_lo):
@@ -516,12 +516,12 @@
         (2, SUBS), (4,), (4, 3), (4, 7), (4, 7), (4, 3), (4,), (), (3,), (7,),
     ]
     sems = [dma(*shape) for shape in pairs for _ in range(2)]
-    panels, sums, groups = pl.pallas_call(
+    panels, sums, inverse = pl.pallas_call(
         functools.partial(gather_kernel, rows_total),
         out_shape=(
             jax.ShapeDtypeStruct((4, 1024, NB), F32),
             jax.ShapeDtypeStruct((4, 32, 8, 512), F32),
-            jax.ShapeDtypeStruct((GROUPS, 8, 128), F32),
+            jax.ShapeDtypeStruct((N, N), F32),
         ),
         in_specs=[any_space],
         out_specs=[any_space] * 3,
@@ -530,24 +530,15 @@
             vmem(4, 1024, NB), vmem(4, 32, 8, 512), vmem(4, 32, 8, 512), vmem(4, 3, 8, 8, 512),
             vmem(4, 8, 8, 512), vmem(4, 7, 8, 512), vmem(4, 32, 8, 512),
             vmem(GROUPS, 8, 128), vmem(GROUPS, 8, 128), vmem(3, forty, 8, 128), vmem(forty, 8, 128),
-            vmem(7, five, 8, 128), vmem(GROUPS, 8, 128),
+            vmem(7, five, 8, 128), vmem(GROUPS, 8, 128), vmem(N, N), vmem(N, N),
             dma(5), dma(9), *sems,
-            dma(3), dma(), dma(7), dma(7), dma(3), dma(3), dma(), dma(),
+            dma(3), dma(), dma(7), dma(7), dma(3), dma(3), dma(4), dma(4),
         ],
         compiler_params=pltpu.CompilerParams(
             collective_id=0, has_side_effects=True, vmem_limit_bytes=56 * 1024 * 1024
         ),
         name="gather",
     )(matrix)
-    inverse = pl.pallas_call(
-        factor_kernel,
-        out_shape=jax.ShapeDtypeStruct((N, N), F32),
-        in_specs=[pl.BlockSpec(memory_space=pltpu.VMEM)],
-        out_specs=pl.BlockSpec(memory_space=pltpu.VMEM),
-        scratch_shapes=[vmem(N, N)],
-        compiler_params=pltpu.CompilerParams(vmem_limit_bytes=32 * 1024 * 1024),
-        name="factor",
-    )(groups)
     tile = 256
     return pl.pallas_call(
         finish_kernel,
@@ -572,7 +563,7 @@
             vmem(N, N, dtype=BF16), vmem(N, N, dtype=BF16),
             vmem(N, 1024, dtype=BF16), vmem(N, 1024, dtype=BF16),
         ],
-        compiler_params=pltpu.CompilerParams(vmem_limit_bytes=48 * 1024 * 1024),
+        compiler_params=pltpu.CompilerParams(vmem_limit_bytes=60 * 1024 * 1024),
         name="finish",
     )(matrix, panels, inverse, sums)
 

time: 129 us -> 105 us (0.81)
  Pallas kernels: 124 us -> 104 us
  local copies, waits for them, and re-layouts: 4.26 us -> 0 us
    pallas_call x1 -> x0, Pallas kernels: 21 us -> none  [on_device(): pl.pallas_call(factor_kernel, out_shape=jax.ShapeDtypeStruct((N, N), F32)...]
    unnamed x6 -> x0, local copies, waits for them, and re-layouts: 4.26 us -> none
where the time goes in v2:
time: 105 us
  Pallas kernels  104 us (99%)
    pallas_call x1, Pallas kernels, on_device(): pl.pallas_call(functools.partial(gather_kernel, rows_total), out_shape=(j...  93.3 us
    pallas_call x1, Pallas kernels, on_device(): pl.pallas_call(finish_kernel, grid=(1024 // tile,), out_shape=(jax.ShapeD...  10.9 us

profile of v2, /device:TPU:9, one launch (start us, length us, event | category | flops | bytes accessed | tf_op | source)
XLA Modules:
  0.0 104.8 jit_solution(9987547599440709271)
XLA Ops:
  0.6 93.3 %gather.1 = (f32[4,1024,128]{2,1,0:T(8,128)}, f32[4,32,8,512]{3,2,1,0:T(8,128)}, f32[512,512]{1,0:T(8,128)}) custom-call(f32[1024,1024]{1,0:T(8,128)} %a.1), custom_call_target="tpu_custom_call" | custom-call | tf_op jit(solution)/shard_map/gather/pallas_call | solution.py:519
  93.9 10.9 %finish.1 = (f32[1024,512]{1,0:T(8,128)}, f32[512,1024]{1,0:T(8,128)}, f32[1024,1024]{1,0:T(8,128)}) custom-call(f32[1024,1024]{1,0:T(8,128)} %a.1, f32[4,1024,128]{2,1,0:T(8,128)} %get-tuple-element.6.p, f32[512,512]{1,0:T(8,128)} %get-tuple-element.7.inv, f32[4,32,8,512]{3,2,1,0:T(8,128)} %get-tuple-element.8.c), custom_call_target="tpu_custom_call" | custom-call | tf_op jit(solution)/shard_map/finish/pallas_call | solution.py:543

commit v3 on v2

--- a/solution.py
+++ b/solution.py
@@ -11,9 +11,14 @@
 F32, BF16 = jnp.float32, jnp.bfloat16
 X, Z, Y = 4, 8, 4
 N, NB = 512, 128
-CHUNKS = 4
-SUBS = 8
-PART = 256
+STEP = 32
+SUBS = N // STEP
+MID, END = 2, 5
+WIDTHS = (128, 128, 128, 64, 64)
+CHUNKS = len(WIDTHS)
+STARTS = [sum(WIDTHS[:k]) for k in range(CHUNKS)]
+READY = [(STARTS[k] + WIDTHS[k]) // STEP - 1 + END for k in range(CHUNKS)]
+SPACING = 4
 BLOCKS = [(i, j) for j in range(4) for i in range(j, 4)]
 GROUPS = 16 * len(BLOCKS)
 
@@ -91,14 +96,20 @@
             inv[b:, :b] = inv[b:, :b] - dot_full(low, inv[a:b, :b], ((1,), (0,)))
 
 
-def gather_kernel(
-    rows_total, a_hbm, p_out, c_out, inv_out,
-    a, a_hi, a_lo, p, c_own, c_sib, c_x, c_s, c_z, c_all,
-    g_own, g_sib, g_x, g_s, g_z, g_all, gram, inv,
-    load_sem, store_sem, p_send, p_recv, cs_send, cs_recv, cx_send, cx_recv, cz_send, cz_recv,
-    caz_send, caz_recv, cax_send, cax_recv, ce_send, ce_recv, gs_send, gs_recv, gx_send, gx_recv,
-    gz_send, gz_recv, gy_send, gy_recv, gaz_send, gaz_recv, gax_send, gax_recv, ge_send, ge_recv,
-):
+def gather_kernel(rows_total, a_hbm, q_out, coeff_out, *scratch):
+    scratch = list(scratch)
+
+    def take(count):
+        taken = scratch[:count]
+        del scratch[:count]
+        return taken
+
+    a, a_hi, a_lo, p, c_full, q, coeff = take(7)
+    c_own, c_sib, c_x, c_s, c_z, c_all = (take(CHUNKS) for _ in range(6))
+    g_own, g_sib, g_x, g_s, g_z, g_all, gram, inv = take(8)
+    load_sem, store_sem, p_send, p_recv, cs_send, cs_recv, cx_send, cx_recv, cz_send, cz_recv = take(10)
+    caz_send, caz_recv, cax_send, cax_recv, ce_send, ce_recv, gs_send, gs_recv, gx_send, gx_recv = take(10)
+    gz_send, gz_recv, gy_send, gy_recv, gaz_send, gaz_recv, gax_send, gax_recv, ge_send, ge_recv = take(10)
     row, y = lax.axis_index("row"), lax.axis_index("col")
     core, z, x = row % 2, (row // 2) % Z, row // (2 * Z)
     piece = x * Z + z
@@ -127,8 +138,7 @@
         pl.semaphore_signal(barrier, inc=1, device_id=friend, device_id_type=MESH)
 
     def p_copy(way, s, step):
-        rows = pl.ds(512 * way + PART * (s % 2), PART)
-        part = p.at[s // 2, rows, :]
+        part = p.at[way, pl.ds(STEP * s, STEP)]
         return remote(part, part, p_send.at[way, s], p_recv.at[way, s], at(x, (y + step) % Y, z, core))
 
     def up(s):
@@ -138,12 +148,12 @@
         return p_copy(1, s, Y - 1)
 
     def cs(k):
-        return [remote(c_own.at[k], c_sib.at[k], cs_send.at[k], cs_recv.at[k], sibling)]
+        return [remote(c_own[k], c_sib[k], cs_send.at[k], cs_recv.at[k], sibling)]
 
     def cx(k):
         return [
             remote(
-                c_own.at[k, pl.ds(x_peer(i) * Z, Z)], c_x.at[k, i - 1],
+                c_own[k].at[pl.ds(x_peer(i) * Z, Z)], c_x[k].at[i - 1],
                 cx_send.at[k, i - 1], cx_recv.at[k, i - 1], at(x_peer(i), y, z, core),
             )
             for i in range(1, X)
@@ -152,7 +162,7 @@
     def cz(k):
         return [
             remote(
-                c_s.at[k, z_peer(i)], c_z.at[k, i - 1],
+                c_s[k].at[z_peer(i)], c_z[k].at[i - 1],
                 cz_send.at[k, i - 1], cz_recv.at[k, i - 1], at(x, y, z_peer(i), core),
             )
             for i in range(1, Z)
@@ -161,21 +171,21 @@
     def caz(k):
         return [
             remote(
-                c_all.at[k, piece], c_all.at[k, piece],
+                c_all[k].at[piece], c_all[k].at[piece],
                 caz_send.at[k, i - 1], caz_recv.at[k, i - 1], at(x, y, z_peer(i), core),
             )
             for i in range(1, Z)
         ]
 
     def cax(k):
-        own = c_all.at[k, pl.ds(x * Z, Z)]
+        own = c_all[k].at[pl.ds(x * Z, Z)]
         return [
             remote(own, own, cax_send.at[k, i - 1], cax_recv.at[k, i - 1], at(x_peer(i), y, z, core))
             for i in range(1, X)
         ]
 
     def ce(k):
-        return [remote(c_all.at[k], c_all.at[k], ce_send.at[k], ce_recv.at[k], sibling)]
+        return [remote(c_all[k], c_all[k], ce_send.at[k], ce_recv.at[k], sibling)]
 
     five, forty = GROUPS // (X * Z), GROUPS // X
 
@@ -237,22 +247,20 @@
         for copy in copies:
             copy.wait_send()
 
-    def p_load(k):
-        return pltpu.make_async_copy(a_hbm.at[:, pl.ds(NB * k, NB)], p.at[k], load_sem.at[1 + k])
-
-    a_load = pltpu.make_async_copy(a_hbm, a, load_sem.at[0])
+    def panel(start, width):
+        rows = slice(start, start + width)
+        return split(jnp.concatenate([p[0, rows, :], p[1, rows, :]], axis=1))
+
+    a_load = pltpu.make_async_copy(a_hbm, a, load_sem)
+    a_load.start()
+    a_load.wait()
 
     @pl.when(y == 0)
     def _():
-        for k in range(CHUNKS):
-            p_load(k).start()
-
-    a_load.start()
-
-    @pl.when(y == 0)
-    def _():
-        for k in range(CHUNKS):
-            p_load(k).wait()
+        for k in range(4):
+            for way in range(2):
+                cols = slice(NB * k, NB * k + NB)
+                p[way, cols, :] = a[512 * way : 512 * way + 512, cols].T
 
     pl.semaphore_wait(barrier, len(friends))
 
@@ -261,7 +269,7 @@
         for s in range(SUBS):
             up(s).start()
             down(s).start()
-        flipped = [split(p[k].T) for k in range(CHUNKS)]
+        flipped = [panel(NB * k, NB) for k in range(4)]
         for b, (i, j) in enumerate(BLOCKS):
             block = dot3(flipped[i], flipped[j], ((1,), (1,)))
             for r in range(16):
@@ -277,7 +285,6 @@
             g_own[...] = g_own[...] + g_sib[...]
             start(gx())
 
-    a_load.wait()
     for r in range(0, 1024, 256):
         high, low = split(a[r : r + 256, :])
         a_hi[r : r + 256, :] = high
@@ -289,55 +296,63 @@
             if t < SUBS:
                 up(t).wait_recv()
                 up(t).start()
-            if 0 <= t - 2 < SUBS:
-                down(t - 2).wait_recv()
+            if 0 <= t - END < SUBS:
+                down(t - END).wait_recv()
 
         @pl.when(y == 2)
         def _():
-            if 0 <= t - 1 < SUBS:
-                up(t - 1).wait_recv()
-                up(t - 1).start()
-                down(t - 1).wait_recv()
-                down(t - 1).start()
+            if 0 <= t - MID < SUBS:
+                up(t - MID).wait_recv()
+                up(t - MID).start()
+                down(t - MID).wait_recv()
+                down(t - MID).start()
 
         @pl.when(y == 3)
         def _():
             if t < SUBS:
                 down(t).wait_recv()
                 down(t).start()
-            if 0 <= t - 2 < SUBS:
-                up(t - 2).wait_recv()
-
-    def p_store(k):
-        return pltpu.make_async_copy(p.at[k], p_out.at[k], store_sem.at[k])
+            if 0 <= t - END < SUBS:
+                up(t - END).wait_recv()
 
     def compute(k):
-        left = split(p[k].T)
+        width, lanes = WIDTHS[k], 4 * WIDTHS[k]
+        left = panel(STARTS[k], width)
         for tile in range(4):
-            lanes = slice(256 * tile, 256 * tile + 256)
-            part = dot3(left, (a_hi[:, lanes], a_lo[:, lanes]), ((1,), (0,)))
-            half, inner = tile // 2, slice(256 * (tile % 2), 256 * (tile % 2) + 256)
-            for r in range(16):
-                c_own[k, 2 * r + half, :, inner] = part[8 * r : 8 * r + 8, :]
-        p_store(k).start()
+            cols = slice(256 * tile, 256 * tile + 256)
+            part = dot3(left, (a_hi[:, cols], a_lo[:, cols]), ((1,), (0,)))
+            size = min(256, lanes)
+            for first in range(256 * tile, 256 * tile + 256, size):
+                inner = slice(first % lanes, first % lanes + size)
+                offset = first - 256 * tile
+                for r in range(width // 8):
+                    c_own[k][r * (1024 // lanes) + first // lanes, :, inner] = part[
+                        8 * r : 8 * r + 8, offset : offset + size
+                    ]
+
+    def unfold(k):
+        lanes = 4 * WIDTHS[k]
+        parts = 1024 // lanes
+        for i in range(X * Z):
+            rows = STARTS[k] + 8 * (i // parts)
+            first = lanes * (i % parts)
+            c_full[rows : rows + 8, first : first + lanes] = c_all[k][i]
 
     def c_stage(k, stage):
-        if not 0 <= k < CHUNKS:
-            return
         if stage == 1:
             arrive(cs(k))
-            c_own[k] = c_own[k] + c_sib[k]
+            c_own[k][...] = c_own[k][...] + c_sib[k][...]
             start(cx(k))
         elif stage == 2:
             arrive(cx(k))
-            c_s[k] = c_own[k, pl.ds(x * Z, Z)] + c_x[k, 0] + (c_x[k, 1] + c_x[k, 2])
+            c_s[k][...] = c_own[k][pl.ds(x * Z, Z)] + c_x[k][0] + (c_x[k][1] + c_x[k][2])
             start(cz(k))
         elif stage == 3:
             arrive(cz(k))
-            total = c_s[k, z]
+            total = c_s[k][z]
             for i in range(Z - 1):
-                total = total + c_z[k, i]
-            c_all[k, piece] = total * (1.0 / rows_total)
+                total = total + c_z[k][i]
+            c_all[k][piece] = total * (1.0 / rows_total)
             start(caz(k))
         elif stage == 4:
             arrive(caz(k))
@@ -345,9 +360,33 @@
         elif stage == 5:
             arrive(cax(k))
             start(ce(k))
+            unfold(k)
+
+    def bases():
+        right = split(inv[...])
+        half = N // 2
+        for way in range(2):
+            rows = slice(512 * way, 512 * way + 512)
+            left = split(p[way].T)
+            q[rows, :half] = dot3(
+                (left[0][:, :half], left[1][:, :half]),
+                (right[0][:half, :half], right[1][:half, :half]),
+                ((1,), (1,)),
+            )
+            q[rows, half:] = dot3(left, (right[0][half:], right[1][half:]), ((1,), (1,)))
+        q_store.start()
+
+    def coefficients(first, last):
+        left = split(inv[first:last, :last])
+        for tile in range(4):
+            cols = slice(256 * tile, 256 * tile + 256)
+            coeff[first:last, cols] = dot3(left, split(c_full[:last, cols]), ((1,), (0,)))
+
+    q_store = pltpu.make_async_copy(q, q_out, store_sem.at[0])
+    coeff_store = pltpu.make_async_copy(coeff, coeff_out, store_sem.at[1])
 
     def g_stage(t):
-        if t == 4:
+        if t == READY[0]:
 
             @pl.when(y == 0)
             def _():
@@ -355,7 +394,7 @@
                 g_s[...] = g_own[pl.ds(x * forty, forty)] + g_x[0] + (g_x[1] + g_x[2])
                 start(gz())
 
-        if t == 6:
+        if t == READY[1]:
 
             @pl.when(y == 0)
             def _():
@@ -366,63 +405,71 @@
                 g_all[pl.ds(piece * five, five)] = total * (1.0 / rows_total)
                 start(gy())
 
-        if t == 8:
+        if t == READY[2] - 1:
 
             @pl.when(y != 0)
             def _():
                 gy()[0].wait_recv()
 
             start(gaz())
-        if t == 10:
+        if t == READY[3]:
             arrive(gaz())
             start(gax())
-        if t == 12:
+        if t == READY[4]:
             arrive(gax())
             for b, (i, j) in enumerate(BLOCKS):
                 for r in range(16):
                     gram[NB * i + 8 * r : NB * i + 8 * r + 8, NB * j : NB * j + NB] = g_all[16 * b + r]
             factor(gram, inv, lambda k: start(ge(k)))
 
-    for t in range(14):
+    due = sorted((READY[k] + 1 + SPACING * (stage - 1), k, stage) for k in range(CHUNKS) for stage in range(1, 6))
+    end = SUBS + END
+    for t in range(end):
         p_step(t)
-        ready = (t - 3) // 2
-        fresh = t >= 3 and t % 2 == 1 and ready < CHUNKS
-        if fresh:
-            compute(ready)
+        fresh = [k for k in range(CHUNKS) if READY[k] == t]
+        for k in fresh:
+            compute(k)
 
         @pl.when(core == 1)
         def _():
-            if fresh:
-                start(cs(ready))
+            for k in fresh:
+                start(cs(k))
             g_stage(t)
 
         @pl.when(core == 0)
         def _():
-            if fresh:
-                c_stage(ready, 1)
-            for stage in range(5, 1, -1):
-                if (t - stage - 2) % 2 == 0:
-                    c_stage((t - stage - 2) // 2, stage)
-
-    inv_store = pltpu.make_async_copy(inv, inv_out, store_sem.at[4])
-
-    def c_store(k):
-        return pltpu.make_async_copy(c_all.at[k], c_out.at[k], store_sem.at[5 + k])
+            for when, k, stage in due:
+                if when == t:
+                    c_stage(k, stage)
+
+    early = [k for k in range(CHUNKS) if STARTS[k] + WIDTHS[k] <= N - NB]
 
     @pl.when(core == 0)
     def _():
-        for k in range(CHUNKS):
-            c_store(k).start()
+        for when, k, stage in due:
+            if when >= end and (k, stage) != (CHUNKS - 1, 5):
+                c_stage(k, stage)
         for k in range(4):
             arrive(ge(k))
-        inv_store.start()
+        bases()
+        coefficients(0, N - NB)
+        c_stage(CHUNKS - 1, 5)
+        coefficients(N - NB, N)
+        coeff_store.start()
 
     @pl.when(core == 1)
     def _():
-        inv_store.start()
+        bases()
+        for k in early:
+            arrive(ce(k))
+            unfold(k)
+        coefficients(0, N - NB)
         for k in range(CHUNKS):
-            arrive(ce(k))
-            c_store(k).start()
+            if k not in early:
+                arrive(ce(k))
+                unfold(k)
+        coefficients(N - NB, N)
+        coeff_store.start()
 
     @pl.when((y == 0) | (y == 1) | (y == 2))
     def _():
@@ -451,50 +498,24 @@
 
         for k in range(CHUNKS):
             sent(cs(k))
+        for k in range(4):
             sent(ge(k))
         sent(gaz() + gax())
 
-    for k in range(CHUNKS):
-        p_store(k).wait()
-        c_store(k).wait()
-    inv_store.wait()
-
-
-def finish_kernel(a, p, inv, c, q, coeff, rest, inv_hi, inv_lo, coeff_hi, coeff_lo):
-    half = N // 2
-
+    q_store.wait()
+    coeff_store.wait()
+
+
+def finish_kernel(a, q_in, coeff_in, q, coeff, rest, coeff_hi, coeff_lo):
     @pl.when(pl.program_id(0) == 0)
     def _():
-        high, low = split(inv[...])
-        inv_hi[...] = high
-        inv_lo[...] = low
-        for tile in range(2):
-            lanes = slice(512 * tile, 512 * tile + 512)
-            sums = [
-                jnp.concatenate([c[k, 2 * r + tile] for k in ks for r in range(16)], axis=0)
-                for ks in ((0, 1), (2, 3))
-            ]
-            right = split(jnp.concatenate(sums, axis=0))
-            upper = dot3(
-                (high[:half, :half], low[:half, :half]), (right[0][:half], right[1][:half]), ((1,), (0,))
-            )
-            lower = dot3((high[half:], low[half:]), right, ((1,), (0,)))
-            for start, part in ((0, upper), (half, lower)):
-                coeff[start : start + half, lanes] = part
-                part_hi, part_lo = split(part)
-                coeff_hi[start : start + half, lanes] = part_hi
-                coeff_lo[start : start + half, lanes] = part_lo
-
-    panels = split(jnp.concatenate([p[k] for k in range(CHUNKS)], axis=1))
-    upper = dot3(
-        (panels[0][:, :half], panels[1][:, :half]),
-        (inv_hi[:half, :half], inv_lo[:half, :half]),
-        ((1,), (1,)),
-    )
-    lower = dot3(panels, (inv_hi[half:, :], inv_lo[half:, :]), ((1,), (1,)))
-    basis = jnp.concatenate([upper, lower], axis=1)
-    q[...] = basis
-    left = split(basis)
+        coeff[...] = coeff_in[...]
+        high, low = split(coeff_in[...])
+        coeff_hi[...] = high
+        coeff_lo[...] = low
+
+    q[...] = q_in[...]
+    left = split(q_in[...])
     for tile in range(2):
         lanes = slice(512 * tile, 512 * tile + 512)
         rest[:, lanes] = a[:, lanes] - dot3(left, (coeff_hi[:, lanes], coeff_lo[:, lanes]), ((1,), (0,)))
@@ -513,25 +534,23 @@
     any_space = pl.BlockSpec(memory_space=pl.ANY)
     five, forty = GROUPS // (X * Z), GROUPS // X
     pairs = [
-        (2, SUBS), (4,), (4, 3), (4, 7), (4, 7), (4, 3), (4,), (), (3,), (7,),
+        (2, SUBS), (CHUNKS,), (CHUNKS, 3), (CHUNKS, 7), (CHUNKS, 7), (CHUNKS, 3), (CHUNKS,), (), (3,), (7,),
     ]
     sems = [dma(*shape) for shape in pairs for _ in range(2)]
-    panels, sums, inverse = pl.pallas_call(
+    sizes = [4 * width for width in WIDTHS]
+    shapes = ((32, 8), (32, 8), (3, 8, 8), (8, 8), (7, 8), (32, 8))
+    basis, coeff = pl.pallas_call(
         functools.partial(gather_kernel, rows_total),
-        out_shape=(
-            jax.ShapeDtypeStruct((4, 1024, NB), F32),
-            jax.ShapeDtypeStruct((4, 32, 8, 512), F32),
-            jax.ShapeDtypeStruct((N, N), F32),
-        ),
+        out_shape=(jax.ShapeDtypeStruct((1024, N), F32), jax.ShapeDtypeStruct((N, 1024), F32)),
         in_specs=[any_space],
-        out_specs=[any_space] * 3,
+        out_specs=[any_space] * 2,
         scratch_shapes=[
             vmem(1024, 1024), vmem(1024, 1024, dtype=BF16), vmem(1024, 1024, dtype=BF16),
-            vmem(4, 1024, NB), vmem(4, 32, 8, 512), vmem(4, 32, 8, 512), vmem(4, 3, 8, 8, 512),
-            vmem(4, 8, 8, 512), vmem(4, 7, 8, 512), vmem(4, 32, 8, 512),
+            vmem(2, 512, 512), vmem(N, 1024), vmem(1024, N), vmem(N, 1024),
+            *[vmem(*shape, size) for shape in shapes for size in sizes],
             vmem(GROUPS, 8, 128), vmem(GROUPS, 8, 128), vmem(3, forty, 8, 128), vmem(forty, 8, 128),
             vmem(7, five, 8, 128), vmem(GROUPS, 8, 128), vmem(N, N), vmem(N, N),
-            dma(5), dma(9), *sems,
+            dma(), dma(2), *sems,
             dma(3), dma(), dma(7), dma(7), dma(3), dma(3), dma(4), dma(4),
         ],
         compiler_params=pltpu.CompilerParams(
@@ -550,22 +569,18 @@
         ),
         in_specs=[
             pl.BlockSpec((tile, 1024), lambda i: (i, 0)),
-            pl.BlockSpec((4, tile, NB), lambda i: (0, i, 0)),
-            pl.BlockSpec((N, N), lambda i: (0, 0)),
-            pl.BlockSpec((4, 32, 8, 512), lambda i: (0, 0, 0, 0)),
+            pl.BlockSpec((tile, N), lambda i: (i, 0)),
+            pl.BlockSpec((N, 1024), lambda i: (0, 0)),
         ],
         out_specs=[
             pl.BlockSpec((tile, N), lambda i: (i, 0)),
             pl.BlockSpec((N, 1024), lambda i: (0, 0)),
             pl.BlockSpec((tile, 1024), lambda i: (i, 0)),
         ],
-        scratch_shapes=[
-            vmem(N, N, dtype=BF16), vmem(N, N, dtype=BF16),
-            vmem(N, 1024, dtype=BF16), vmem(N, 1024, dtype=BF16),
-        ],
+        scratch_shapes=[vmem(N, 1024, dtype=BF16), vmem(N, 1024, dtype=BF16)],
         compiler_params=pltpu.CompilerParams(vmem_limit_bytes=60 * 1024 * 1024),
         name="finish",
-    )(matrix, panels, inverse, sums)
+    )(matrix, basis, coeff)
 
 
 def solution(mesh):

time: 105 us -> 88.5 us (0.84); the launches traced: 105 us -> 86.8 us
  Pallas kernels: 104 us -> 86.2 us
    pallas_call x1, Pallas kernels: 93.3 us -> 77.1 us  [on_device(): pl.pallas_call(functools.partial(gather_kernel, rows_total), out_shape=(j...]
    pallas_call x1, Pallas kernels: 10.9 us -> 9.08 us  [on_device(): pl.pallas_call(finish_kernel, grid=(1024 // tile,), out_shape=(jax.ShapeD...]
where the time goes in v3:
time: 88.5 us; the launch traced here: 86.8 us
  Pallas kernels  86.2 us (97%)
    pallas_call x1, Pallas kernels, on_device(): pl.pallas_call(functools.partial(gather_kernel, rows_total), out_shape=(j...  77.1 us
    pallas_call x1, Pallas kernels, on_device(): pl.pallas_call(finish_kernel, grid=(1024 // tile,), out_shape=(jax.ShapeD...  9.08 us

profile of v3, /device:TPU:9, one launch (start us, length us, event | category | flops | bytes accessed | tf_op | source)
XLA Modules:
  0.0 86.8 jit_solution(9413651509832296959)
XLA Ops:
  0.6 77.1 %gather.1 = (f32[1024,512]{1,0:T(8,128)}, f32[512,1024]{1,0:T(8,128)}) custom-call(f32[1024,1024]{1,0:T(8,128)} %a.1), custom_call_target="tpu_custom_call" | custom-call | tf_op jit(solution)/shard_map/gather/pallas_call | solution.py:542
  77.7 9.1 %finish.1 = (f32[1024,512]{1,0:T(8,128)}, f32[512,1024]{1,0:T(8,128)}, f32[1024,1024]{1,0:T(8,128)}) custom-call(f32[1024,1024]{1,0:T(8,128)} %a.1, f32[1024,512]{1,0:T(8,128)} %get-tuple-element.5.q_in, f32[512,1024]{1,0:T(8,128)} %get-tuple-element.6.coeff_in), custom_call_target="tpu_custom_call" | custom-call | tf_op jit(solution)/shard_map/finish/pallas_call | solution.py:562

commit v4 on v3

--- a/solution.py
+++ b/solution.py
@@ -18,6 +18,8 @@
 CHUNKS = len(WIDTHS)
 STARTS = [sum(WIDTHS[:k]) for k in range(CHUNKS)]
 READY = [(STARTS[k] + WIDTHS[k]) // STEP - 1 + END for k in range(CHUNKS)]
+SHORT = [width == 32 for width in WIDTHS]
+STAGES = [4 if short else 5 for short in SHORT]
 SPACING = 4
 BLOCKS = [(i, j) for j in range(4) for i in range(j, 4)]
 GROUPS = 16 * len(BLOCKS)
@@ -29,10 +31,10 @@
 
 
 def dot3(left, right, dims):
-    dot = functools.partial(
-        lax.dot_general, dimension_numbers=(dims, ((), ())), preferred_element_type=F32
-    )
-    return dot(left[0], right[0]) + (dot(left[0], right[1]) + dot(left[1], right[0]))
+    (left_dim,), (right_dim,) = dims
+    left = jnp.concatenate([left[0], left[0], left[1]], axis=left_dim)
+    right = jnp.concatenate([right[0], right[1], right[0]], axis=right_dim)
+    return lax.dot_general(left, right, (dims, ((), ())), preferred_element_type=F32)
 
 
 def dot_full(left, right, dims):
@@ -88,12 +90,12 @@
         own = jnp.concatenate(leaf([gram[a + 8 * i : a + 8 * i + 8, a:b] for i in range(16)]), axis=0)
         inv[a:b, a:b] = own
         if k:
-            inv[a:b, :a] = dot_full(own, inv[a:b, :a], ((1,), (0,)))
+            inv[a:b, :a] = dot3(split(own), split(inv[a:b, :a]), ((1,), (0,)))
         done(k)
         if k < 3:
             low = dot_full(gram[b:, a:b], own, ((1,), (1,)))
             gram[b:, b:] = gram[b:, b:] - dot_full(low, low, ((1,), (1,)))
-            inv[b:, :b] = inv[b:, :b] - dot_full(low, inv[a:b, :b], ((1,), (0,)))
+            inv[b:, :b] = inv[b:, :b] - dot3(split(low), split(inv[a:b, :b]), ((1,), (0,)))
 
 
 def gather_kernel(rows_total, a_hbm, q_out, coeff_out, *scratch):
@@ -104,7 +106,7 @@
         del scratch[:count]
         return taken
 
-    a, a_hi, a_lo, p, c_full, q, coeff = take(7)
+    a, a_hi, a_lo, p, p_hi, p_lo, c_full, q, coeff = take(9)
     c_own, c_sib, c_x, c_s, c_z, c_all = (take(CHUNKS) for _ in range(6))
     g_own, g_sib, g_x, g_s, g_z, g_all, gram, inv = take(8)
     load_sem, store_sem, p_send, p_recv, cs_send, cs_recv, cx_send, cx_recv, cz_send, cz_recv = take(10)
@@ -160,6 +162,12 @@
         ]
 
     def cz(k):
+        if SHORT[k]:
+            own = c_z[k].at[z]
+            return [
+                remote(own, own, cz_send.at[k, i - 1], cz_recv.at[k, i - 1], at(x, y, z_peer(i), core))
+                for i in range(1, Z)
+            ]
         return [
             remote(
                 c_s[k].at[z_peer(i)], c_z[k].at[i - 1],
@@ -251,9 +259,14 @@
         rows = slice(start, start + width)
         return split(jnp.concatenate([p[0, rows, :], p[1, rows, :]], axis=1))
 
-    a_load = pltpu.make_async_copy(a_hbm, a, load_sem)
-    a_load.start()
-    a_load.wait()
+    def a_load(half):
+        cols = pl.ds(512 * half, 512)
+        return pltpu.make_async_copy(a_hbm.at[:, cols], a.at[:, cols], load_sem.at[half])
+
+    a_load(0).start()
+    a_load(1).start()
+    a_load(0).wait()
+    pl.semaphore_wait(barrier, len(friends))
 
     @pl.when(y == 0)
     def _():
@@ -261,14 +274,9 @@
             for way in range(2):
                 cols = slice(NB * k, NB * k + NB)
                 p[way, cols, :] = a[512 * way : 512 * way + 512, cols].T
-
-    pl.semaphore_wait(barrier, len(friends))
-
-    @pl.when(y == 0)
-    def _():
-        for s in range(SUBS):
-            up(s).start()
-            down(s).start()
+            for s in range(NB // STEP * k, NB // STEP * (k + 1)):
+                up(s).start()
+                down(s).start()
         flipped = [panel(NB * k, NB) for k in range(4)]
         for b, (i, j) in enumerate(BLOCKS):
             block = dot3(flipped[i], flipped[j], ((1,), (1,)))
@@ -285,6 +293,7 @@
             g_own[...] = g_own[...] + g_sib[...]
             start(gx())
 
+    a_load(1).wait()
     for r in range(0, 1024, 256):
         high, low = split(a[r : r + 256, :])
         a_hi[r : r + 256, :] = high
@@ -330,6 +339,13 @@
                         8 * r : 8 * r + 8, offset : offset + size
                     ]
 
+    def turn(start):
+        for way in range(2):
+            rows, cols = slice(512 * way, 512 * way + 512), slice(start, start + NB)
+            high, low = split(p[way, cols, :].T)
+            p_hi[rows, cols] = high
+            p_lo[rows, cols] = low
+
     def unfold(k):
         lanes = 4 * WIDTHS[k]
         parts = 1024 // lanes
@@ -345,8 +361,16 @@
             start(cx(k))
         elif stage == 2:
             arrive(cx(k))
-            c_s[k][...] = c_own[k][pl.ds(x * Z, Z)] + c_x[k][0] + (c_x[k][1] + c_x[k][2])
+            part = c_s[k] if not SHORT[k] else c_z[k].at[z]
+            part[...] = c_own[k][pl.ds(x * Z, Z)] + c_x[k][0] + (c_x[k][1] + c_x[k][2])
             start(cz(k))
+        elif stage == 3 and SHORT[k]:
+            arrive(cz(k))
+            total = c_z[k][0]
+            for i in range(1, Z):
+                total = total + c_z[k][i]
+            c_all[k][pl.ds(x * Z, Z)] = total * (1.0 / rows_total)
+            start(cax(k))
         elif stage == 3:
             arrive(cz(k))
             total = c_s[k][z]
@@ -354,10 +378,10 @@
                 total = total + c_z[k][i]
             c_all[k][piece] = total * (1.0 / rows_total)
             start(caz(k))
-        elif stage == 4:
+        elif stage == 4 and not SHORT[k]:
             arrive(caz(k))
             start(cax(k))
-        elif stage == 5:
+        else:
             arrive(cax(k))
             start(ce(k))
             unfold(k)
@@ -367,7 +391,7 @@
         half = N // 2
         for way in range(2):
             rows = slice(512 * way, 512 * way + 512)
-            left = split(p[way].T)
+            left = p_hi[rows, :], p_lo[rows, :]
             q[rows, :half] = dot3(
                 (left[0][:, :half], left[1][:, :half]),
                 (right[0][:half, :half], right[1][:half, :half]),
@@ -383,7 +407,10 @@
             coeff[first:last, cols] = dot3(left, split(c_full[:last, cols]), ((1,), (0,)))
 
     q_store = pltpu.make_async_copy(q, q_out, store_sem.at[0])
-    coeff_store = pltpu.make_async_copy(coeff, coeff_out, store_sem.at[1])
+
+    def coeff_store(late):
+        rows = pl.ds((N - NB) * late, NB if late else N - NB)
+        return pltpu.make_async_copy(coeff.at[rows], coeff_out.at[rows], store_sem.at[1 + late])
 
     def g_stage(t):
         if t == READY[0]:
@@ -415,14 +442,14 @@
         if t == READY[3]:
             arrive(gaz())
             start(gax())
-        if t == READY[4]:
+        if t == READY[-1]:
             arrive(gax())
             for b, (i, j) in enumerate(BLOCKS):
                 for r in range(16):
                     gram[NB * i + 8 * r : NB * i + 8 * r + 8, NB * j : NB * j + NB] = g_all[16 * b + r]
             factor(gram, inv, lambda k: start(ge(k)))
 
-    due = sorted((READY[k] + 1 + SPACING * (stage - 1), k, stage) for k in range(CHUNKS) for stage in range(1, 6))
+    due = sorted((READY[k] + 1 + SPACING * (stage - 1), k, stage) for k in range(CHUNKS) for stage in range(1, STAGES[k] + 1))
     end = SUBS + END
     for t in range(end):
         p_step(t)
@@ -434,6 +461,8 @@
         def _():
             for k in fresh:
                 start(cs(k))
+                if (STARTS[k] + WIDTHS[k]) % NB == 0:
+                    turn(STARTS[k] + WIDTHS[k] - NB)
             g_stage(t)
 
         @pl.when(core == 0)
@@ -441,21 +470,24 @@
             for when, k, stage in due:
                 if when == t:
                     c_stage(k, stage)
+            for k in fresh:
+                if (STARTS[k] + WIDTHS[k]) % NB == 0:
+                    turn(STARTS[k] + WIDTHS[k] - NB)
 
     early = [k for k in range(CHUNKS) if STARTS[k] + WIDTHS[k] <= N - NB]
 
     @pl.when(core == 0)
     def _():
         for when, k, stage in due:
-            if when >= end and (k, stage) != (CHUNKS - 1, 5):
+            if when >= end:
                 c_stage(k, stage)
         for k in range(4):
             arrive(ge(k))
         bases()
         coefficients(0, N - NB)
-        c_stage(CHUNKS - 1, 5)
+        coeff_store(0).start()
         coefficients(N - NB, N)
-        coeff_store.start()
+        coeff_store(1).start()
 
     @pl.when(core == 1)
     def _():
@@ -464,12 +496,13 @@
             arrive(ce(k))
             unfold(k)
         coefficients(0, N - NB)
+        coeff_store(0).start()
         for k in range(CHUNKS):
             if k not in early:
                 arrive(ce(k))
                 unfold(k)
         coefficients(N - NB, N)
-        coeff_store.start()
+        coeff_store(1).start()
 
     @pl.when((y == 0) | (y == 1) | (y == 2))
     def _():
@@ -488,7 +521,7 @@
             sent(gs())
 
         for k in range(CHUNKS):
-            sent(cx(k) + cz(k) + caz(k) + cax(k) + ce(k))
+            sent(cx(k) + cz(k) + ([] if SHORT[k] else caz(k)) + cax(k) + ce(k))
 
     @pl.when(core == 1)
     def _():
@@ -503,7 +536,8 @@
         sent(gaz() + gax())
 
     q_store.wait()
-    coeff_store.wait()
+    coeff_store(0).wait()
+    coeff_store(1).wait()
 
 
 def finish_kernel(a, q_in, coeff_in, q, coeff, rest, coeff_hi, coeff_lo):
@@ -539,6 +573,12 @@
     sems = [dma(*shape) for shape in pairs for _ in range(2)]
     sizes = [4 * width for width in WIDTHS]
     shapes = ((32, 8), (32, 8), (3, 8, 8), (8, 8), (7, 8), (32, 8))
+    short_shapes = (*shapes[:4], (8, 8, 8), shapes[5])
+    sums = [
+        vmem(*(short_shape if short else shape), size)
+        for shape, short_shape in zip(shapes, short_shapes)
+        for size, short in zip(sizes, SHORT)
+    ]
     basis, coeff = pl.pallas_call(
         functools.partial(gather_kernel, rows_total),
         out_shape=(jax.ShapeDtypeStruct((1024, N), F32), jax.ShapeDtypeStruct((N, 1024), F32)),
@@ -546,11 +586,11 @@
         out_specs=[any_space] * 2,
         scratch_shapes=[
             vmem(1024, 1024), vmem(1024, 1024, dtype=BF16), vmem(1024, 1024, dtype=BF16),
-            vmem(2, 512, 512), vmem(N, 1024), vmem(1024, N), vmem(N, 1024),
-            *[vmem(*shape, size) for shape in shapes for size in sizes],
+            vmem(2, 512, 512), vmem(1024, N, dtype=BF16), vmem(1024, N, dtype=BF16), vmem(N, 1024), vmem(1024, N), vmem(N, 1024),
+            *sums,
             vmem(GROUPS, 8, 128), vmem(GROUPS, 8, 128), vmem(3, forty, 8, 128), vmem(forty, 8, 128),
             vmem(7, five, 8, 128), vmem(GROUPS, 8, 128), vmem(N, N), vmem(N, N),
-            dma(), dma(2), *sems,
+            dma(2), dma(3), *sems,
             dma(3), dma(), dma(7), dma(7), dma(3), dma(3), dma(4), dma(4),
         ],
         compiler_params=pltpu.CompilerParams(

time: 88.5 us -> 86.4 us (0.976)
  Pallas kernels: 86.2 us -> 84.9 us
    pallas_call x1, Pallas kernels: 77.1 us -> 75.8 us  [on_device(): pl.pallas_call(functools.partial(gather_kernel, rows_total), out_shape=(j...]
where the time goes in v4:
time: 86.4 us; the launch traced here: 85.5 us
  Pallas kernels  84.9 us (98%)
    pallas_call x1, Pallas kernels, on_device(): pl.pallas_call(functools.partial(gather_kernel, rows_total), out_shape=(j...  75.8 us
    pallas_call x1, Pallas kernels, on_device(): pl.pallas_call(finish_kernel, grid=(1024 // tile,), out_shape=(jax.ShapeD...  9.1 us

profile of v4, /device:TPU:9, one launch (start us, length us, event | category | flops | bytes accessed | tf_op | source)
XLA Modules:
  0.0 85.5 jit_solution(11627736756769373377)
XLA Ops:
  0.6 75.8 %gather.1 = (f32[1024,512]{1,0:T(8,128)}, f32[512,1024]{1,0:T(8,128)}) custom-call(f32[1024,1024]{1,0:T(8,128)} %a.1), custom_call_target="tpu_custom_call" | custom-call | tf_op jit(solution)/shard_map/gather/pallas_call | solution.py:582
  76.4 9.1 %finish.1 = (f32[1024,512]{1,0:T(8,128)}, f32[512,1024]{1,0:T(8,128)}, f32[1024,1024]{1,0:T(8,128)}) custom-call(f32[1024,1024]{1,0:T(8,128)} %a.1, f32[1024,512]{1,0:T(8,128)} %get-tuple-element.5.q_in, f32[512,1024]{1,0:T(8,128)} %get-tuple-element.6.coeff_in), custom_call_target="tpu_custom_call" | custom-call | tf_op jit(solution)/shard_map/finish/pallas_call | solution.py:602

commit v5 on v4

--- a/solution.py
+++ b/solution.py
@@ -598,7 +598,7 @@
         ),
         name="gather",
     )(matrix)
-    tile = 256
+    tile = 512
     return pl.pallas_call(
         finish_kernel,
         grid=(1024 // tile,),

time: 86.4 us -> 86.2 us (level)
  no operation moved by 1% of the time
where the time goes in v5:
time: 86.2 us; the launch traced here: 85.4 us
  Pallas kernels  84.7 us (98%)
    pallas_call x1, Pallas kernels, on_device(): pl.pallas_call(functools.partial(gather_kernel, rows_total), out_shape=(j...  75.8 us
    pallas_call x1, Pallas kernels, on_device(): pl.pallas_call(finish_kernel, grid=(1024 // tile,), out_shape=(jax.ShapeD...  8.93 us

profile of v5, /device:TPU:9, one launch (start us, length us, event | category | flops | bytes accessed | tf_op | source)
XLA Modules:
  0.0 85.4 jit_solution(6152013589632239510)
XLA Ops:
  0.6 75.8 %gather.1 = (f32[1024,512]{1,0:T(8,128)}, f32[512,1024]{1,0:T(8,128)}) custom-call(f32[1024,1024]{1,0:T(8,128)} %a.1), custom_call_target="tpu_custom_call" | custom-call | tf_op jit(solution)/shard_map/gather/pallas_call | solution.py:582
  76.4 8.9 %finish.1 = (f32[1024,512]{1,0:T(8,128)}, f32[512,1024]{1,0:T(8,128)}, f32[1024,1024]{1,0:T(8,128)}) custom-call(f32[1024,1024]{1,0:T(8,128)} %a.1, f32[1024,512]{1,0:T(8,128)} %get-tuple-element.5.q_in, f32[512,1024]{1,0:T(8,128)} %get-tuple-element.6.coeff_in), custom_call_target="tpu_custom_call" | custom-call | tf_op jit(solution)/shard_map/finish/pallas_call | solution.py:602
